TPU v7x, 32 devices: a whole 2x2x4 slice. The times are simulated.
32 devices in a mesh: layer: 8 (over z, core), feat: 4 (over y, x).
Axes of the slice: x: 2, y: 2, z: 4, core: 2. Of those that a mesh axis runs over, the one named last changes fastest.
Arguments:
- attn_heads: bfloat16 [8, 768, 2048], P('layer', None, 'feat'), may hold values from -6 to 6
- out_proj: bfloat16 [8, 2048, 2048], P('layer', 'feat'), may hold values from -0.125 to 0.125
- resid_pre: bfloat16 [8, 768, 2048], P('layer'), may hold values from -6 to 6
- enc_weight: bfloat16 [8, 2048, 16384], P('layer', None, 'feat'), may hold values from -0.03125 to 0.03125
- enc_bias: float32 [16384], P('feat'), may hold values from -4 to 4
- dec_weight: bfloat16 [8, 16384, 2048], P('layer', 'feat'), may hold values from -0.09375 to 0.09375
- dec_bias: float32 [8, 2048], P('layer', 'feat'), may hold values from -3 to 3
Outputs:
- features: float32 [768, 16384], P('layer', 'feat')
- rebuilt: float32 [8, 768, 2048], P('layer', None, 'feat')
All inputs are finite; a program needn't handle non-finite values.
Results may differ from a plain program's by a relative error of at most 0.0035.
Values may be sent and summed in bfloat16 or wider, within the bound.
No kernel may reach another device: no remote copies, remote signals or barrier semaphores. Data moves between devices by JAX's collectives and lax.ppermute only.
A program may use at most 128 MiB of HBM per device.

v0:
```python
import jax
import jax.numpy as jnp
from jax import lax
from jax.sharding import PartitionSpec as P


def per_device(attn_heads, out_proj, resid_pre, enc_weight, enc_bias, dec_weight, dec_bias):
    head_rows = attn_heads[0]
    out_weight = out_proj[0]
    residual = resid_pre[0]
    encoder = enc_weight[0]
    decoder = dec_weight[0]
    partial_value = jnp.dot(head_rows, out_weight, preferred_element_type=jnp.float32)
    projected = lax.psum(partial_value, "feat")
    hidden = (residual.astype(jnp.float32) + projected).astype(jnp.bfloat16)
    pre_part = jnp.dot(hidden, encoder, preferred_element_type=jnp.float32)
    pre_own = (
        lax.psum_scatter(pre_part, "layer", scatter_dimension=0, tiled=True) + enc_bias[None, :]
    )
    own_feats = jnp.maximum(pre_own, 0.0)
    recon_part = jnp.dot(
        lax.all_gather(own_feats.astype(jnp.bfloat16), "layer", axis=0, tiled=True),
        decoder,
        preferred_element_type=jnp.float32,
    )
    rebuilt = (
        lax.psum_scatter(recon_part, "feat", scatter_dimension=1, tiled=True) + dec_bias[0][None, :]
    )
    return (own_feats, rebuilt[None])


def solution(mesh):
    return jax.shard_map(
        per_device,
        mesh=mesh,
        in_specs=(
            P("layer", None, "feat"),
            P("layer", "feat", None),
            P("layer", None, None),
            P("layer", None, "feat"),
            P("feat"),
            P("layer", "feat", None),
            P("layer", "feat"),
        ),
        out_specs=(P("layer", "feat"), P("layer", None, "feat")),
        check_vma=False,
    )
```

profile of v0, /device:TPU:0, one launch (start us, length us, event | category | flops | bytes accessed | tf_op | source)
XLA Modules:
  0.0 472.2 jit_solution(10630355062078301174)
XLA Ops:
  7.2 0.0 copy-start
  7.2 0.0 all-reduce.2.cloned.1.call-start
  7.2 1.5 copy-done
  8.8 5.6 %fusion.7 = f32[768,2048]{1,0:T(8,128)} fusion(bf16[1,512,2048]{2,1,0:T(8,128)(2,1)S(1)} %copy-done, bf16[1,768,512]{2,1,0:T(8,128)(2,1)} %param.7), kind=kOutput, calls=%fused_computation.7 | convolution fusion | flops 1610612736 | bytes 9175040 | tf_op jit(solution)/shard_map/dot_general | solution.py:13
  14.4 0.0 all-reduce.2.cloned.1.call-update
  14.4 0.0 reduce-scatter.3.cloned.1.call-start
  14.4 141.3 %all-reduce.2.cloned.1.call-done = f32[768,2048]{1,0:T(8,128)} async-done(((f32[768,2048]{1,0:T(8,128)}), f32[768,2048]{1,0:T(8,128)}) %all-reduce.2.cloned.1.call-update) | async-done | bytes 6291472 | tf_op jit(solution)/shard_map/psum | solution.py:14
  155.7 22.1 %fusion.2 = f32[768,4096]{1,0:T(8,128)} fusion(bf16[1,2048,4096]{2,1,0:T(8,128)(2,1)} %param.10, f32[768,2048]{1,0:T(8,128)} %all-reduce.2.cloned.1.call-done, bf16[1,768,2048]{2,1,0:T(8,128)(2,1)} %param.9), kind=kOutput, calls=%fused_computation.2 | convolution fusion | flops 12889620480 | bytes 38797312 | tf_op jit(solution)/shard_map/dot_general | solution.py:16
  177.8 0.0 copy-start.2
  177.8 0.0 reduce-scatter.3.cloned.1.call-update
  177.8 0.0 all-gather.2.cloned.1.call-start
  177.8 129.3 %reduce-scatter.3.cloned.1.call-done = f32[96,4096]{1,0:T(8,128)} async-done(((f32[768,4096]{1,0:T(8,128)}), f32[96,4096]{1,0:T(8,128)}) %reduce-scatter.3.cloned.1.call-update) | async-done | bytes 1572880 | tf_op jit(solution)/shard_map/reduce_scatter | solution.py:18
  307.2 0.0 copy-done.2
  307.2 3.0 fusion.10
  310.2 0.0 all-gather.2.cloned.1.call-update
  310.2 0.0 reduce-scatter.5.cloned.1.call-start
  310.3 63.2 %all-gather.2.cloned.1.call-done = bf16[768,4096]{1,0:T(8,128)(2,1)} async-done(((bf16[96,4096]{1,0:T(8,128)(2,1)}), bf16[768,4096]{1,0:T(8,128)(2,1)}) %all-gather.2.cloned.1.call-update) | async-done | bytes 6291472 | tf_op jit(solution)/shard_map/all_gather | solution.py:22
  373.5 0.0 copy-start.1
  373.5 20.4 %fusion = f32[768,2048]{1,0:T(8,128)} fusion(bf16[768,4096]{1,0:T(8,128)(2,1)} %all-gather.2.cloned.1.call-done, bf16[1,4096,2048]{2,1,0:T(8,128)(2,1)} %param.12), kind=kOutput, calls=%fused_computation | convolution fusion | flops 12884901888 | bytes 29360128 | tf_op jit(solution)/shard_map/dot_general | solution.py:21
  393.9 0.0 reduce-scatter.5.cloned.1.call-update
  393.9 69.0 %reduce-scatter.5.cloned.1.call-done = f32[768,512]{1,0:T(8,128)} async-done(((f32[768,2048]{1,0:T(8,128)}), f32[768,512]{1,0:T(8,128)}) %reduce-scatter.5.cloned.1.call-update) | async-done | bytes 1572880 | tf_op jit(solution)/shard_map/reduce_scatter | solution.py:27
  462.9 0.0 copy-done.3
  462.9 2.7 add_bitcast_fusion
  465.6 0.0 copy-done.1
  (1 shorter events, 0.0 us)
Async XLA Ops:
  7.2 1.6 copy-start
  7.2 148.5 %all-reduce.2.cloned.1.call-start = ((), (), s32[]{:S(2)}) async-start(), calls=%async_computation.2 | async-start | bytes 12582912 | tf_op jit(solution)/shard_map/psum | solution.py:14
  14.4 292.8 %reduce-scatter.3.cloned.1.call-start = ((), (), s32[]{:S(2)}) async-start(), calls=%async_computation.3 | async-start | bytes 14155776 | tf_op jit(solution)/shard_map/reduce_scatter | solution.py:18
  177.8 129.4 %copy-start.2 = (f32[4096]{0:T(1024)S(1)}, f32[4096]{0:T(1024)}, u32[]{:S(2)}) copy-start(f32[4096]{0:T(1024)} %param.11) | copy-start | bytes 49156
  177.8 195.7 %all-gather.2.cloned.1.call-start = ((), (), s32[]{:S(2)}) async-start(), calls=%async_computation.4 | async-start | bytes 7077888 | tf_op jit(solution)/shard_map/all_gather | solution.py:22
  310.2 152.7 %reduce-scatter.5.cloned.1.call-start = ((), (), s32[]{:S(2)}) async-start(), calls=%async_computation.5 | async-start | bytes 7864320 | tf_op jit(solution)/shard_map/reduce_scatter | solution.py:27
  373.5 92.2 %copy-start.1 = (bf16[1,512,2048]{2,1,0:T(8,128)(2,1)S(1)}, bf16[1,512,2048]{2,1,0:T(8,128)(2,1)}, u32[]{:S(2)}) copy-start(bf16[1,512,2048]{2,1,0:T(8,128)(2,1)} %param.8) | copy-start | bytes 6291460
  393.9 69.1 %copy-start.3 = (f32[1,512]{1,0:T(1,128)S(1)}, f32[1,512]{1,0:T(1,128)}, u32[]{:S(2)}) copy-start(f32[1,512]{1,0:T(1,128)} %param.13) | copy-start | bytes 6148
Sparse Core Ops, SparseCore 0:
  14.5 141.1 all-reduce.1
  177.9 129.2 reduce-scatter.2
  310.3 63.0 all-gather.1
  394.0 68.8 reduce-scatter.4
where the time goes:
time: 472 us
  waiting for transfers between devices  403 us (85%)
  matrix products  48 us (10%)
  between operations  13.8 us (3%)
  other arithmetic  5.75 us (1%)
    psum x1, waiting for transfers between devices, per_device(): projected = lax.psum(partial_value, 'feat')  141 us
    reduce_scatter x1, waiting for transfers between devices, per_device(): lax.psum_scatter(pre_part, 'layer', scatter_dimension=0, tiled=True)  129 us
    reduce_scatter x1, waiting for transfers between devices, per_device(): lax.psum_scatter(recon_part, 'feat', scatter_dimension=1, tiled=True)  69 us
    all_gather x1, waiting for transfers between devices, per_device(): lax.all_gather(own_feats.astype(jnp.bfloat16), 'layer', axis=0, tiled=True)  63.2 us
    dot_general x1, matrix products, per_device(): pre_part = jnp.dot(hidden, encoder, preferred_element_type=jnp.float32)  22.1 us
    dot_general x1, matrix products, per_device(): jnp.dot(lax.all_gather(own_feats.astype(jnp.bfloat16), 'layer', axis=0, t...  20.4 us
  transfers between devices with their start and end apart: 4, of which 4 were waited for; matrix products, arithmetic and copies ran while one was open for 0% of the time, Pallas kernels for 0%

commit v1 on v0

v1 whole, which is shorter than its diff:
```python
import functools

import jax
import jax.numpy as jnp
from jax import lax
from jax.experimental import pallas as pl
from jax.experimental.pallas import tpu as pltpu
from jax.sharding import PartitionSpec as P

F32 = jnp.float32
BF16 = jnp.bfloat16
VMEM_LIMIT = 6 * 2**20
UNIT = 16
PLANS = {
    6: (
        ((1,), (1,), (1, 1), (1, 1)),
        ((0, 1, 2), (3, 4), (5,)),
        (0, 3, 1, 0, 2, 0, 1, 0, 2, 1, 3, 4, 2, 4, 1, 3, 2, 4, 5, 3, 4, 5, 6, 4, 5, 6, 8, 5, 4, 6, 8, 7, 6, 7, 8, 5, 7, 6, 9, 8, 9, 7, 6, 5, 8, 10, 9, 7, 8, 9, 7, 10, 9, 11, 9, 12, 11, 10, 12, 11, 12),
    ),
}


def like(shape, dtype):
    return jax.ShapeDtypeStruct(shape, dtype)


class Core:
    def __init__(self, info):
        self.info = info
        self.last = info

    def run(self, name, body, out_shape, *args, far=0, scratch=(), flops=0):
        vmem = pl.BlockSpec(memory_space=pltpu.VMEM)
        args = lax.optimization_barrier((*args, self.last))[:-1]
        spaces = [pltpu.HBM] * far + [pltpu.VMEM] * (len(args) - far)

        moved = sum(a.size * a.dtype.itemsize for a in (*args, *out_shape))
        outs = pl.pallas_call(
            body,
            in_specs=[pl.BlockSpec(memory_space=pltpu.SMEM)]
            + [pl.BlockSpec(memory_space=space) for space in spaces],
            out_specs=[vmem] * len(out_shape),
            out_shape=list(out_shape),
            scratch_shapes=list(scratch),
            compiler_params=pltpu.CompilerParams(vmem_limit_bytes=VMEM_LIMIT),
            cost_estimate=pl.CostEstimate(flops=flops, bytes_accessed=moved, transcendentals=0),
            name=name,
        )(self.info, *map(pltpu.with_memory_space_constraint, args, spaces))
        self.last = min(outs, key=lambda a: a.size)
        return outs

    def fuse(self, function, *args):
        args = lax.optimization_barrier((*args, self.last))[:-1]
        self.last = function(*args)
        return self.last


def project(core, heads, residual, weight, off, r, span, F):
    K, D = weight.shape
    rows = span * r
    tile = min(1024, D)
    first = off == 0

    def body(info_ref, a_ref, res_ref, w_ref, keep, send, x, res, sems, *own):
        copies = [
            pltpu.make_async_copy(
                a_ref.at[pl.ds(info_ref[3 + m] * span, span), off : off + r],
                x.at[m * span : (m + 1) * span],
                sems.at[m],
            )
            for m in range(F)
        ]
        copies.append(
            pltpu.make_async_copy(
                res_ref.at[pl.ds(info_ref[3] * span, span), off : off + r], res, sems.at[F]
            )
        )
        if first:
            copies.append(pltpu.make_async_copy(w_ref, own[0], sems.at[F + 1]))
            w_ref = own[0]
        for copy in copies:
            copy.start()
        for copy in copies:
            copy.wait()

        @pl.loop(0, D // tile)
        def _(i):
            cols = pl.ds(pl.multiple_of(i * tile, tile), tile)
            acc = jnp.dot(x[...].reshape(F * rows, K), w_ref[:, cols], preferred_element_type=F32)
            for m in range(F):
                part = acc[m * rows : (m + 1) * rows]
                if m % 2:
                    send[m // 2, :, cols] = part.astype(send.dtype)
                elif m:
                    keep[m // 2, :, cols] = part
                else:
                    keep[0, :, cols] = part + res[:, :, cols].astype(F32).reshape(rows, tile)

    half = (F // 2, rows, D)
    return core.run(
        "project",
        body,
        [like(half, F32), like(half, BF16)],
        heads,
        residual,
        weight,
        far=3 if first else 2,
        scratch=[
            pltpu.VMEM((F * span, r, K), BF16),
            pltpu.VMEM((span, r, D), BF16),
            pltpu.SemaphoreType.DMA((F + 2,)),
        ]
        + [pltpu.VMEM((K, D), BF16)] * first,
        flops=2 * F * rows * K * D,
    )


def encode(core, near, far, weight, off, r, L, F):
    D, FL = weight.shape
    tile = min(1024, FL)
    span = L // F
    group = near.shape[1] // span

    def body(info_ref, near_ref, far_ref, w_ref, keep, send, x):
        me = info_ref[1]
        for m in range(F):
            for i in range(span):
                at = pl.multiple_of((info_ref[3 + m] * span + i) * r, r)
                rows = slice(i * group + off, i * group + off + r)
                x[pl.ds(at, r), :] = (far_ref if m % 2 else near_ref)[m // 2, rows, :]

        @pl.loop(0, FL // tile)
        def _(i):
            cols = pl.ds(pl.multiple_of(i * tile, tile), tile)
            acc = jnp.dot(x[...], w_ref[:, cols], preferred_element_type=F32)
            for p in range(L):
                m = me ^ p
                part = acc[p * r : (p + 1) * r]

                @pl.when(m % 2 == 0)
                def _():
                    keep[m // 2, :, cols] = part

                @pl.when(m % 2 == 1)
                def _():
                    send[m // 2, :, cols] = part.astype(send.dtype)

    half = (L // 2, r, FL)
    return core.run(
        "encode",
        body,
        [like(half, F32), like(half, BF16)],
        near,
        far,
        weight,
        scratch=[pltpu.VMEM((L * r, D), BF16)],
        flops=2 * L * r * D * FL,
    )


def decode(core, chunks, weight, L, F):
    FL, D = weight.shape
    wide = D // F
    sizes = [near.shape[1] for near, far in chunks]
    rows = L * sum(sizes)

    def body(info_ref, *refs):
        w_ref, keep, send, x = refs[2 * len(chunks) :]
        start = 0
        for c, r in enumerate(sizes):
            for m in range(L):
                at = pl.multiple_of(start + (info_ref[1] ^ m) * r, UNIT)
                x[pl.ds(at, r), :] = refs[2 * c + m % 2][m // 2]
            start += L * r

        @pl.loop(0, F // 2)
        def _(i):
            def product(m):
                cols = pl.ds(pl.multiple_of(info_ref[3 + m] * wide, wide), wide)
                return jnp.dot(x[...], w_ref[:, cols], preferred_element_type=F32)

            send[i] = product(2 * i + 1).astype(send.dtype)
            keep[i] = product(2 * i)

    half = (F // 2, rows, wide)
    return core.run(
        "decode",
        body,
        [like(half, F32), like(half, BF16)],
        *[a for pair in chunks for a in pair],
        weight,
        scratch=[pltpu.VMEM((rows, FL), BF16)],
        flops=2 * rows * D * FL,
    )


def total(parts):
    out = parts[0].astype(F32)
    for part in parts[1:]:
        out = out + part.astype(F32)
    return out


def reduce_steps(core, keep, send, exchange, stages, last_type=BF16):
    terms = [keep, exchange(send, 0)]
    yield
    for s in range(1, stages):
        sent_as = last_type if s == stages - 1 else BF16
        moved = core.fuse(lambda *ts: total([t[1::2] for t in ts]).astype(sent_as), *terms)
        terms = [t[0::2] for t in terms] + [exchange(moved, s)]
        yield
    return terms


def gather_steps(core, own, exchange, stages):
    near = own
    for s in range(stages - 1, 0, -1):
        far = exchange(near, s)
        yield
        shape = (2 * near.shape[0], *near.shape[1:])
        near = core.fuse(
            lambda a, b: jnp.stack([a, b], axis=1).reshape(shape), near, far
        )
    far = exchange(near, 0)
    yield
    return near, far


class Work:
    def __init__(self, core, L, F, arrays):
        self.core, self.L, self.F, self.arrays = core, L, F, arrays
        self.fbits, self.lbits = F.bit_length() - 1, L.bit_length() - 1
        self.hidden, self.coded, self.features, self.rebuilt = {}, {}, {}, {}

    def over_feat(self, a, s):
        pairs = []
        for l in range(self.L):
            bit = 1 << (self.fbits - 1 - s if l % 2 else s)
            pairs += [(l * self.F + i, l * self.F + (i ^ bit)) for i in range(self.F)]
        return lax.ppermute(a, ("layer", "feat"), pairs)

    def over_layer(self, a, s):
        return lax.ppermute(a, "layer", [(l, l ^ (1 << s)) for l in range(self.L)])

    def prepare(self, group, off, r, wide):
        core, span = self.core, self.L // self.F
        heads, residual, out_weight = self.arrays[:3]
        keep, send = project(core, heads, residual, out_weight, off, r, span, self.F)
        terms = yield from reduce_steps(core, keep, send, self.over_feat, self.fbits, wide)
        hidden = core.fuse(lambda *ts: total(ts).astype(BF16), *terms)
        self.hidden[group] = yield from gather_steps(core, hidden, self.over_feat, self.fbits)

    def activate(self, chunk, group, off, r):
        core = self.core
        encoder, enc_bias = self.arrays[3:5]
        keep, send = encode(core, *self.hidden[group], encoder, off, r, self.L, self.F)
        terms = yield from reduce_steps(core, keep, send, self.over_layer, self.lbits)
        feats = core.fuse(lambda *ts: jnp.maximum(total(ts) + enc_bias, 0.0), *terms)
        self.features[chunk] = feats[0]
        coded = feats.astype(BF16)
        self.coded[chunk] = yield from gather_steps(core, coded, self.over_layer, self.lbits)

    def rebuild(self, chunks, wide):
        core = self.core
        decoder, dec_bias = self.arrays[5:]
        pairs = [self.coded[c] for c in chunks]
        keep, send = decode(core, pairs, decoder, self.L, self.F)
        terms = yield from reduce_steps(core, keep, send, self.over_feat, self.fbits, wide)
        out = core.fuse(lambda *ts: total(ts) + dec_bias, *terms)[0]
        start = 0
        for c, (near, far) in zip(chunks, pairs):
            r = near.shape[1]
            self.rebuilt[c] = out[start : start + self.L * r].reshape(self.L, r, -1)
            start += self.L * r


def plan(units):
    if units in PLANS:
        return PLANS[units]
    groups = [(1,)] * units
    return groups, [(c,) for c in range(units)], []


def fast(L, Fn, heads, out_weight, residual, encoder, enc_bias, decoder, dec_bias):
    T, K = heads.shape
    D = out_weight.shape[1]
    per, span = T // L, L // Fn
    f = lax.axis_index("feat")
    layer = lax.axis_index("layer")
    fbits, lbits = Fn.bit_length() - 1, L.bit_length() - 1
    places = []
    for m in range(Fn):
        back = sum(1 << (fbits - 1 - s) for s in range(fbits) if m >> s & 1)
        places.append(f ^ jnp.where(layer % 2 == 0, m, back))
    core = Core(jnp.stack([f, layer, layer % 2, *places]).astype(jnp.int32))
    arrays = (
        heads.reshape(L, per, K),
        residual.reshape(L, per, D),
        out_weight,
        encoder,
        enc_bias[None, None],
        decoder,
        dec_bias[None, None],
    )
    work = Work(core, L, Fn, arrays)
    groups, joins, order = plan(per // UNIT)
    start = 0
    prepares, activates = [], []
    for g, sizes in enumerate(groups):
        prepares.append(work.prepare(g, start * UNIT, sum(sizes) * UNIT, F32 if g else BF16))
        off = 0
        for units in sizes:
            activates.append(work.activate(len(activates), g, off, units * UNIT))
            off += units * UNIT
        start += sum(sizes)
    rebuilds = [work.rebuild(j, BF16 if j == joins[-1] else F32) for j in joins]
    runs = prepares + activates + rebuilds
    left = [2 * work.fbits] * len(prepares) + [2 * work.lbits] * len(activates)
    left += [work.fbits + 1] * len(rebuilds)
    order = order or [c for c in range(len(runs)) for _ in range(left[c])]
    for c in order:
        next(runs[c], None)
        left[c] -= 1
        if left[c] == 0:
            next(runs[c], None)
    features = jnp.concatenate([work.features[c] for c in range(len(activates))], axis=0)
    rebuilt = jnp.concatenate([work.rebuilt[c] for c in range(len(activates))], axis=1)
    return features, rebuilt.reshape(1, T, -1)


def plain(heads, out_weight, residual, encoder, enc_bias, decoder, dec_bias):
    part = jnp.dot(heads, out_weight, preferred_element_type=F32)
    hidden = (residual.astype(F32) + lax.psum(part, "feat")).astype(BF16)
    pre = jnp.dot(hidden, encoder, preferred_element_type=F32)
    own = lax.psum_scatter(pre, "layer", scatter_dimension=0, tiled=True) + enc_bias[None, :]
    own = jnp.maximum(own, 0.0)
    coded = lax.all_gather(own.astype(BF16), "layer", axis=0, tiled=True)
    recon = jnp.dot(coded, decoder, preferred_element_type=F32)
    out = lax.psum_scatter(recon, "feat", scatter_dimension=1, tiled=True) + dec_bias[None, :]
    return own, out[None]


def per_device(L, Fn, attn_heads, out_proj, resid_pre, enc_weight, enc_bias, dec_weight, dec_bias):
    args = (attn_heads[0], out_proj[0], resid_pre[0], enc_weight[0], enc_bias, dec_weight[0], dec_bias[0])
    powers = L & (L - 1) == 0 and Fn & (Fn - 1) == 0
    if powers and Fn >= 2 and L >= 2 and L % Fn == 0 and args[0].shape[0] % (L * UNIT) == 0:
        return fast(L, Fn, *args)
    return plain(*args)


def solution(mesh):
    return jax.shard_map(
        functools.partial(per_device, mesh.shape["layer"], mesh.shape["feat"]),
        mesh=mesh,
        in_specs=(
            P("layer", None, "feat"),
            P("layer", "feat", None),
            P("layer", None, None),
            P("layer", None, "feat"),
            P("feat"),
            P("layer", "feat", None),
            P("layer", "feat"),
        ),
        out_specs=(P("layer", "feat"), P("layer", None, "feat")),
        check_vma=False,
    )
```

time: 472 us -> 206 us (0.44)
  waiting for transfers between devices: 403 us -> 83 us
  starting transfers between devices: 0.16 us -> 61.2 us
  Pallas kernels: 0 us -> 53.3 us
  matrix products: 48 us -> 0 us
  between operations: 13.8 us -> 2.07 us
    reduce_scatter x2 -> x0, waiting for transfers between devices: 198 us -> none  [the longest x1 129 us: per_device(): lax.psum_scatter(pre_part, 'layer', scatter_dimension=0, tiled=True)]
    psum x1 -> x0, waiting for transfers between devices: 141 us -> none  [per_device(): projected = lax.psum(partial_value, 'feat')]
    ppermute x0 -> x58, waiting for transfers between devices: none -> 83 us  [the longest x36 43.5 us: over_layer(): return lax.ppermute(a, 'layer', [(l, l ^ 1 << s) for l in range(self.L)])]
    all_gather x1 -> x0, waiting for transfers between devices: 63.2 us -> none  [per_device(): lax.all_gather(own_feats.astype(jnp.bfloat16), 'layer', axis=0, tiled=True)]
    ppermute x0 -> x58, starting transfers between devices: none -> 61.2 us  [the longest x22 31.8 us: over_feat(): return lax.ppermute(a, ('layer', 'feat'), pairs)]
    pallas_call x0 -> x13, Pallas kernels: none -> 53.3 us  [run(): pl.pallas_call(body, in_specs=[pl.BlockSpec(memory_space=pltpu.SMEM)] + [...]
    dot_general x3 -> x0, matrix products: 48 us -> none  [the longest x1 22.1 us: per_device(): pre_part = jnp.dot(hidden, encoder, preferred_element_type=jnp.float32)]
  transfers between devices with their start and end apart: 4 -> 58, of which waited for: 4 -> 26; matrix products, arithmetic and copies ran while one was open for 0% -> 2% of each run, Pallas kernels for 0% -> 24%
where the time goes in v1:
time: 206 us
  waiting for transfers between devices  83 us (40%)
  starting transfers between devices  61.2 us (30%)
  Pallas kernels  53.3 us (26%)
  local copies, waits for them, and re-layouts  3.66 us (2%)
  other arithmetic  2.71 us (1%)
  between operations  2.07 us (1%)
    pallas_call x13, Pallas kernels, run(): pl.pallas_call(body, in_specs=[pl.BlockSpec(memory_space=pltpu.SMEM)] + [...  53.3 us
    ppermute x36, waiting for transfers between devices, over_layer(): return lax.ppermute(a, 'layer', [(l, l ^ 1 << s) for l in range(self.L)])  43.5 us
    ppermute x22, waiting for transfers between devices, over_feat(): return lax.ppermute(a, ('layer', 'feat'), pairs)  39.5 us
    ppermute x22, starting transfers between devices, over_feat(): return lax.ppermute(a, ('layer', 'feat'), pairs)  31.8 us
    ppermute x36, starting transfers between devices, over_layer(): return lax.ppermute(a, 'layer', [(l, l ^ 1 << s) for l in range(self.L)])  29.3 us
  transfers between devices with their start and end apart: 58, of which 26 were waited for; matrix products, arithmetic and copies ran while one was open for 2% of the time, Pallas kernels for 24%

profile of v1, /device:TPU:0, one launch (start us, length us, event | category | flops | bytes accessed | tf_op | source)
XLA Modules:
  0.0 205.9 jit_solution(16052511836460091040)
XLA Ops:
  0.7 3.3 %project.4 = (f32[2,32,2048]{2,1,0:T(8,128)S(1)}, bf16[2,32,2048]{2,1,0:T(8,128)(2,1)S(1)}) custom-call(s32[7]{0:T(128)S(1)} %stack.172.info_ref, bf16[8,96,512]{2,1,0:T(8,128)(2,1)} %bitcast.122, bf16[8,96,2048]{2,1,0:T(8,128)(2,1)} %bitcast.118, bf16[512,2048]{1,0:T(8,128)(2,1)} %bitcast.102), custom_call_target="tpu_custom_call" | custom-call | flops 268435456 | bytes 6815744 | tf_op jit(solution)/shard_map/project/pallas_call | solution.py:38
  4.0 3.0 %collective-permute-start = (bf16[2,32,2048]{2,1,0:T(8,128)(2,1)S(1)}, bf16[2,32,2048]{2,1,0:T(8,128)(2,1)S(1)}, u32[]{:S(2)}, u32[]{:S(2)}) collective-permute-start(bf16[2,32,2048]{2,1,0:T(8,128)(2,1)S(1)} %get-tuple-element.198), channel_id=1, source_target_pairs={{0,1},{1,0},{2,3},{3,2},{4,6},{5,7},{6,4},{7,5},{8,9},{9,8},{10,11... | collective-permute-start | bytes 786440 | tf_op jit(solution)/shard_map/ppermute | solution.py:240
  21.9 4.3 %collective-permute-done.2 = bf16[1,32,2048]{2,1,0:T(8,128)(2,1)S(1)} collective-permute-done((bf16[1,32,2048]{2,1,0:T(8,128)(2,1)S(1)}, bf16[1,32,2048]{2,1,0:T(8,128)(2,1)S(1)}, u32[]{:S(2)}, u32[]{:S(2)}) %collective-permute-start.2) | collective-permute-done | bytes 131104 | tf_op jit(solution)/shard_map/ppermute | solution.py:240
  27.8 6.6 %collective-permute-done.7 = bf16[2,64,2048]{2,1,0:T(8,128)(2,1)S(1)} collective-permute-done((bf16[2,64,2048]{2,1,0:T(8,128)(2,1)S(1)}, bf16[2,64,2048]{2,1,0:T(8,128)(2,1)S(1)}, u32[]{:S(2)}, u32[]{:S(2)}) %collective-permute-start.7) | collective-permute-done | bytes 524320 | tf_op jit(solution)/shard_map/ppermute | solution.py:240
  37.3 4.2 %encode.6 = (f32[4,16,4096]{2,1,0:T(8,128)S(1)}, bf16[4,16,4096]{2,1,0:T(8,128)(2,1)S(1)}) custom-call(s32[7]{0:T(128)S(1)} %stack.172.info_ref, bf16[2,32,2048]{2,1,0:T(8,128)(2,1)S(1)} %maximum_bitcast_fusion.2.near_ref, bf16[2,32,2048]{2,1,0:T(8,128)(2,1)S(1)} %collective-permute-done.4.far_ref, bf16[2048,4096]{1,0:T(8,128)(2,1)S(1)} %bitcast.91), custom_call_target="tpu_custom_call" | custom-call | flops 2147483648 | bytes 18874368 | tf_op jit(solution)/shard_map/encode/pallas_call | solution.py:38
  41.7 3.2 %collective-permute-start.13 = (bf16[1,32,2048]{2,1,0:T(8,128)(2,1)S(1)}, bf16[1,32,2048]{2,1,0:T(8,128)(2,1)S(1)}, u32[]{:S(2)}, u32[]{:S(2)}) collective-permute-start(bf16[1,32,2048]{2,1,0:T(8,128)(2,1)S(1)} %add_convert_fusion.15), channel_id=1, source_target_pairs={{0,2},{1,3},{2,0},{3,1},{4,5},{5,4},{6,7},{7,6},{8,10},{9,11},{10,... | collective-permute-start | bytes 393224 | tf_op jit(solution)/shard_map/ppermute | solution.py:240
  50.2 6.6 %collective-permute-done.12 = f32[1,64,2048]{2,1,0:T(8,128)S(1)} collective-permute-done((f32[1,64,2048]{2,1,0:T(8,128)S(1)}, f32[1,64,2048]{2,1,0:T(8,128)S(1)}, u32[]{:S(2)}, u32[]{:S(2)}) %collective-permute-start.12) | collective-permute-done | bytes 524320 | tf_op jit(solution)/shard_map/ppermute | solution.py:240
  63.8 4.2 %encode.7 = (f32[4,16,4096]{2,1,0:T(8,128)S(1)}, bf16[4,16,4096]{2,1,0:T(8,128)(2,1)S(1)}) custom-call(s32[7]{0:T(128)S(1)} %stack.172.info_ref, bf16[2,32,2048]{2,1,0:T(8,128)(2,1)S(1)} %maximum_bitcast_fusion.3.near_ref, bf16[2,32,2048]{2,1,0:T(8,128)(2,1)S(1)} %collective-permute-done.16.far_ref, bf16[2048,4096]{1,0:T(8,128)(2,1)S(1)} %bitcast.92), custom_call_target="tpu_custom_call" | custom-call | flops 2147483648 | bytes 18874368 | tf_op jit(solution)/shard_map/encode/pallas_call | solution.py:38
  70.1 3.8 %collective-permute-start.18 = (bf16[2,16,4096]{2,1,0:T(8,128)(2,1)S(1)}, bf16[2,16,4096]{2,1,0:T(8,128)(2,1)S(1)}, u32[]{:S(2)}, u32[]{:S(2)}) collective-permute-start(bf16[2,16,4096]{2,1,0:T(8,128)(2,1)S(1)} %add_convert_fusion.4), channel_id=1, source_target_pairs={{0,8},{4,12},{8,0},{12,4},{16,24},{20,28},{24,16},{28,20},{1,9},{5... | collective-permute-start | bytes 786440 | tf_op jit(solution)/shard_map/ppermute | solution.py:243
  74.0 4.2 %encode.8 = (f32[4,16,4096]{2,1,0:T(8,128)S(1)}, bf16[4,16,4096]{2,1,0:T(8,128)(2,1)S(1)}) custom-call(s32[7]{0:T(128)S(1)} %stack.172.info_ref, bf16[2,64,2048]{2,1,0:T(8,128)(2,1)S(1)} %maximum_bitcast_fusion.near_ref, bf16[2,64,2048]{2,1,0:T(8,128)(2,1)S(1)} %collective-permute-done.20.far_ref, bf16[2048,4096]{1,0:T(8,128)(2,1)S(1)} %bitcast.93), custom_call_target="tpu_custom_call" | custom-call | flops 2147483648 | bytes 19398656 | tf_op jit(solution)/shard_map/encode/pallas_call | solution.py:38
  86.2 4.2 %encode.9 = (f32[4,16,4096]{2,1,0:T(8,128)S(1)}, bf16[4,16,4096]{2,1,0:T(8,128)(2,1)S(1)}) custom-call(s32[7]{0:T(128)S(1)} %stack.172.info_ref, bf16[2,64,2048]{2,1,0:T(8,128)(2,1)S(1)} %maximum_bitcast_fusion.1.near_ref, bf16[2,64,2048]{2,1,0:T(8,128)(2,1)S(1)} %collective-permute-done.22.far_ref, bf16[2048,4096]{1,0:T(8,128)(2,1)S(1)} %bitcast.94), custom_call_target="tpu_custom_call" | custom-call | flops 2147483648 | bytes 19398656 | tf_op jit(solution)/shard_map/encode/pallas_call | solution.py:38
  92.9 4.7 %collective-permute-done.24 = bf16[2,16,4096]{2,1,0:T(8,128)(2,1)S(1)} collective-permute-done((bf16[2,16,4096]{2,1,0:T(8,128)(2,1)S(1)}, bf16[2,16,4096]{2,1,0:T(8,128)(2,1)S(1)}, u32[]{:S(2)}, u32[]{:S(2)}) %collective-permute-start.24) | collective-permute-done | bytes 262176 | tf_op jit(solution)/shard_map/ppermute | solution.py:243
  100.0 4.2 %encode.10 = (f32[4,16,4096]{2,1,0:T(8,128)S(1)}, bf16[4,16,4096]{2,1,0:T(8,128)(2,1)S(1)}) custom-call(s32[7]{0:T(128)S(1)} %stack.172.info_ref, bf16[2,64,2048]{2,1,0:T(8,128)(2,1)S(1)} %maximum_bitcast_fusion.near_ref, bf16[2,64,2048]{2,1,0:T(8,128)(2,1)S(1)} %collective-permute-done.20.far_ref, bf16[2048,4096]{1,0:T(8,128)(2,1)S(1)} %bitcast.95), custom_call_target="tpu_custom_call" | custom-call | flops 2147483648 | bytes 19398656 | tf_op jit(solution)/shard_map/encode/pallas_call | solution.py:38
  112.8 11.5 %collective-permute-done.29 = bf16[2,16,4096]{2,1,0:T(8,128)(2,1)S(1)} collective-permute-done((bf16[2,16,4096]{2,1,0:T(8,128)(2,1)S(1)}, bf16[2,16,4096]{2,1,0:T(8,128)(2,1)S(1)}, u32[]{:S(2)}, u32[]{:S(2)}) %collective-permute-start.29) | collective-permute-done | bytes 262176 | tf_op jit(solution)/shard_map/ppermute | solution.py:243
  126.8 4.4 %encode.11 = (f32[4,16,4096]{2,1,0:T(8,128)S(1)}, bf16[4,16,4096]{2,1,0:T(8,128)(2,1)S(1)}) custom-call(s32[7]{0:T(128)S(1)} %stack.172.info_ref, bf16[2,64,2048]{2,1,0:T(8,128)(2,1)S(1)} %maximum_bitcast_fusion.1.near_ref, bf16[2,64,2048]{2,1,0:T(8,128)(2,1)S(1)} %collective-permute-done.22.far_ref, bf16[2048,4096]{1,0:T(8,128)(2,1)S(1)} %bitcast.96), custom_call_target="tpu_custom_call" | custom-call | flops 2147483648 | bytes 19398656 | tf_op jit(solution)/shard_map/encode/pallas_call | solution.py:38
  137.5 4.6 %collective-permute-done.42 = bf16[1,16,4096]{2,1,0:T(8,128)(2,1)S(1)} collective-permute-done((bf16[1,16,4096]{2,1,0:T(8,128)(2,1)S(1)}, bf16[1,16,4096]{2,1,0:T(8,128)(2,1)S(1)}, u32[]{:S(2)}, u32[]{:S(2)}) %collective-permute-start.42) | collective-permute-done | bytes 131104 | tf_op jit(solution)/shard_map/ppermute | solution.py:243
  142.3 3.1 %collective-permute-done.36 = bf16[2,16,4096]{2,1,0:T(8,128)(2,1)S(1)} collective-permute-done((bf16[2,16,4096]{2,1,0:T(8,128)(2,1)S(1)}, bf16[2,16,4096]{2,1,0:T(8,128)(2,1)S(1)}, u32[]{:S(2)}, u32[]{:S(2)}) %collective-permute-start.36) | collective-permute-done | bytes 262176 | tf_op jit(solution)/shard_map/ppermute | solution.py:243
  145.4 7.7 %decode.3 = (f32[2,384,512]{2,1,0:T(8,128)S(1)}, bf16[2,384,512]{2,1,0:T(8,128)(2,1)S(1)}) custom-call(s32[7]{0:T(128)S(1)} %stack.172.info_ref, bf16[4,16,4096]{2,1,0:T(8,128)(2,1)S(1)} %bitcast.113, bf16[4,16,4096]{2,1,0:T(8,128)(2,1)S(1)} %collective-permute-done.37.refs_1_, bf16[4,16,4096]{2,1,0:T(8,128)(2,1)S(1)} %bitcast.117, ...), custom_call_target="tpu_custom_call" | custom-call | flops 6442450944 | bytes 22282240 | tf_op jit(solution)/shard_map/decode/pallas_call | solution.py:38
  157.8 3.8 %collective-permute-done.43 = bf16[1,16,4096]{2,1,0:T(8,128)(2,1)S(1)} collective-permute-done((bf16[1,16,4096]{2,1,0:T(8,128)(2,1)S(1)}, bf16[1,16,4096]{2,1,0:T(8,128)(2,1)S(1)}, u32[]{:S(2)}, u32[]{:S(2)}) %collective-permute-start.43) | collective-permute-done | bytes 131104 | tf_op jit(solution)/shard_map/ppermute | solution.py:243
  163.0 3.0 %collective-permute-done.47 = bf16[2,16,4096]{2,1,0:T(8,128)(2,1)S(1)} collective-permute-done((bf16[2,16,4096]{2,1,0:T(8,128)(2,1)S(1)}, bf16[2,16,4096]{2,1,0:T(8,128)(2,1)S(1)}, u32[]{:S(2)}, u32[]{:S(2)}) %collective-permute-start.47) | collective-permute-done | bytes 262176 | tf_op jit(solution)/shard_map/ppermute | solution.py:243
  171.6 5.4 %decode.4 = (f32[2,256,512]{2,1,0:T(8,128)S(1)}, bf16[2,256,512]{2,1,0:T(8,128)(2,1)S(1)}) custom-call(s32[7]{0:T(128)S(1)} %stack.172.info_ref, bf16[4,16,4096]{2,1,0:T(8,128)(2,1)S(1)} %bitcast.109, bf16[4,16,4096]{2,1,0:T(8,128)(2,1)S(1)} %collective-permute-done.49.refs_1_, bf16[4,16,4096]{2,1,0:T(8,128)(2,1)S(1)} %bitcast.107, ...), custom_call_target="tpu_custom_call" | custom-call | flops 4294967296 | bytes 20447232 | tf_op jit(solution)/shard_map/decode/pallas_call | solution.py:38
  178.5 7.8 %collective-permute-done.52 = bf16[2,256,512]{2,1,0:T(8,128)(2,1)S(1)} collective-permute-done((bf16[2,256,512]{2,1,0:T(8,128)(2,1)S(1)}, bf16[2,256,512]{2,1,0:T(8,128)(2,1)S(1)}, u32[]{:S(2)}, u32[]{:S(2)}) %collective-permute-start.52) | collective-permute-done | bytes 524320 | tf_op jit(solution)/shard_map/ppermute | solution.py:240
  186.3 3.2 %decode.5 = (f32[2,128,512]{2,1,0:T(8,128)S(1)}, bf16[2,128,512]{2,1,0:T(8,128)(2,1)S(1)}) custom-call(s32[7]{0:T(128)S(1)} %stack.172.info_ref, bf16[4,16,4096]{2,1,0:T(8,128)(2,1)S(1)} %bitcast.111, bf16[4,16,4096]{2,1,0:T(8,128)(2,1)S(1)} %collective-permute-done.54.refs_1_, bf16[4096,2048]{1,0:T(8,128)(2,1)S(1)} %bitcast.101), custom_call_target="tpu_custom_call" | custom-call | flops 2147483648 | bytes 18612224 | tf_op jit(solution)/shard_map/decode/pallas_call | solution.py:38
  192.6 7.0 %collective-permute-done.56 = bf16[2,128,512]{2,1,0:T(8,128)(2,1)S(1)} collective-permute-done((bf16[2,128,512]{2,1,0:T(8,128)(2,1)S(1)}, bf16[2,128,512]{2,1,0:T(8,128)(2,1)S(1)}, u32[]{:S(2)}, u32[]{:S(2)}) %collective-permute-start.56) | collective-permute-done | bytes 262176 | tf_op jit(solution)/shard_map/ppermute | solution.py:240
  (300 shorter events, 85.6 us)
Async XLA Ops:
  14.6 21.7 %collective-permute-start.5 = (bf16[2,64,2048]{2,1,0:T(8,128)(2,1)S(1)}, bf16[2,64,2048]{2,1,0:T(8,128)(2,1)S(1)}, u32[]{:S(2)}, u32[]{:S(2)}) collective-permute-start(bf16[2,64,2048]{2,1,0:T(8,128)(2,1)S(1)} %get-tuple-element.221), channel_id=1, source_target_pairs={{0,1},{1,0},{2,3},{3,2},{4,6},{5,7},{6,4},{7,5},{8,9},{9,8},{10,11... | collective-permute-start | bytes 1572872 | tf_op jit(solution)/shard_map/ppermute | solution.py:240
  19.0 15.4 %collective-permute-start.7 = (bf16[2,64,2048]{2,1,0:T(8,128)(2,1)S(1)}, bf16[2,64,2048]{2,1,0:T(8,128)(2,1)S(1)}, u32[]{:S(2)}, u32[]{:S(2)}) collective-permute-start(bf16[2,64,2048]{2,1,0:T(8,128)(2,1)S(1)} %get-tuple-element.222), channel_id=1, source_target_pairs={{0,1},{1,0},{2,3},{3,2},{4,6},{5,7},{6,4},{7,5},{8,9},{9,8},{10,11... | collective-permute-start | bytes 1572872 | tf_op jit(solution)/shard_map/ppermute | solution.py:240
  21.2 15.1 %collective-permute-start.6 = (f32[1,32,2048]{2,1,0:T(8,128)S(1)}, f32[1,32,2048]{2,1,0:T(8,128)S(1)}, u32[]{:S(2)}, u32[]{:S(2)}) collective-permute-start(f32[1,32,2048]{2,1,0:T(8,128)S(1)} %convert_add_fusion.4), channel_id=1, source_target_pairs={{0,2},{1,3},{2,0},{3,1},{4,5},{5,4},{6,7},{7,6},{8,10},{9,11},{10,... | collective-permute-start | bytes 786440 | tf_op jit(solution)/shard_map/ppermute | solution.py:240
  45.1 14.5 %collective-permute-start.11 = (bf16[1,64,2048]{2,1,0:T(8,128)(2,1)S(1)}, bf16[1,64,2048]{2,1,0:T(8,128)(2,1)S(1)}, u32[]{:S(2)}, u32[]{:S(2)}) collective-permute-start(bf16[1,64,2048]{2,1,0:T(8,128)(2,1)S(1)} %add_convert_fusion.7), channel_id=1, source_target_pairs={{0,2},{1,3},{2,0},{3,1},{4,5},{5,4},{6,7},{7,6},{8,10},{9,11},{10,... | collective-permute-start | bytes 786440 | tf_op jit(solution)/shard_map/ppermute | solution.py:240
  47.2 13.9 %collective-permute-start.10 = (bf16[2,16,4096]{2,1,0:T(8,128)(2,1)S(1)}, bf16[2,16,4096]{2,1,0:T(8,128)(2,1)S(1)}, u32[]{:S(2)}, u32[]{:S(2)}) collective-permute-start(bf16[2,16,4096]{2,1,0:T(8,128)(2,1)S(1)} %add_convert_fusion.6), channel_id=1, source_target_pairs={{0,8},{4,12},{8,0},{12,4},{16,24},{20,28},{24,16},{28,20},{1,9},{5... | collective-permute-start | bytes 786440 | tf_op jit(solution)/shard_map/ppermute | solution.py:243
  48.7 15.1 %collective-permute-start.16 = (bf16[2,32,2048]{2,1,0:T(8,128)(2,1)S(1)}, bf16[2,32,2048]{2,1,0:T(8,128)(2,1)S(1)}, u32[]{:S(2)}, u32[]{:S(2)}) collective-permute-start(bf16[2,32,2048]{2,1,0:T(8,128)(2,1)S(1)} %maximum_bitcast_fusion.3.near_ref), channel_id=1, source_target_pairs={{0,1},{1,0},{2,3},{3,2},{4,6},{5,7},{6,4},{7,5},{8,9},{9,8},{10,11... | collective-permute-start | bytes 786440 | tf_op jit(solution)/shard_map/ppermute | solution.py:240
  59.7 14.2 %collective-permute-start.20 = (bf16[2,64,2048]{2,1,0:T(8,128)(2,1)S(1)}, bf16[2,64,2048]{2,1,0:T(8,128)(2,1)S(1)}, u32[]{:S(2)}, u32[]{:S(2)}) collective-permute-start(bf16[2,64,2048]{2,1,0:T(8,128)(2,1)S(1)} %maximum_bitcast_fusion.near_ref), channel_id=1, source_target_pairs={{0,1},{1,0},{2,3},{3,2},{4,6},{5,7},{6,4},{7,5},{8,9},{9,8},{10,11... | collective-permute-start | bytes 1572872 | tf_op jit(solution)/shard_map/ppermute | solution.py:240
  68.2 17.9 %collective-permute-start.22 = (bf16[2,64,2048]{2,1,0:T(8,128)(2,1)S(1)}, bf16[2,64,2048]{2,1,0:T(8,128)(2,1)S(1)}, u32[]{:S(2)}, u32[]{:S(2)}) collective-permute-start(bf16[2,64,2048]{2,1,0:T(8,128)(2,1)S(1)} %maximum_bitcast_fusion.1.near_ref), channel_id=1, source_target_pairs={{0,1},{1,0},{2,3},{3,2},{4,6},{5,7},{6,4},{7,5},{8,9},{9,8},{10,11... | collective-permute-start | bytes 1572872 | tf_op jit(solution)/shard_map/ppermute | solution.py:240
  70.1 12.4 %collective-permute-start.18 = (bf16[2,16,4096]{2,1,0:T(8,128)(2,1)S(1)}, bf16[2,16,4096]{2,1,0:T(8,128)(2,1)S(1)}, u32[]{:S(2)}, u32[]{:S(2)}) collective-permute-start(bf16[2,16,4096]{2,1,0:T(8,128)(2,1)S(1)} %add_convert_fusion.4), channel_id=1, source_target_pairs={{0,8},{4,12},{8,0},{12,4},{16,24},{20,28},{24,16},{28,20},{1,9},{5... | collective-permute-start | bytes 786440 | tf_op jit(solution)/shard_map/ppermute | solution.py:243
  79.4 12.1 %collective-permute-start.25 = (bf16[2,16,4096]{2,1,0:T(8,128)(2,1)S(1)}, bf16[2,16,4096]{2,1,0:T(8,128)(2,1)S(1)}, u32[]{:S(2)}, u32[]{:S(2)}) collective-permute-start(bf16[2,16,4096]{2,1,0:T(8,128)(2,1)S(1)} %maximum_bitcast_fusion.4), channel_id=1, source_target_pairs={{0,8},{4,12},{8,0},{12,4},{16,24},{20,28},{24,16},{28,20},{1,9},{5... | collective-permute-start | bytes 786440 | tf_op jit(solution)/shard_map/ppermute | solution.py:243
  84.1 13.5 %collective-permute-start.24 = (bf16[2,16,4096]{2,1,0:T(8,128)(2,1)S(1)}, bf16[2,16,4096]{2,1,0:T(8,128)(2,1)S(1)}, u32[]{:S(2)}, u32[]{:S(2)}) collective-permute-start(bf16[2,16,4096]{2,1,0:T(8,128)(2,1)S(1)} %add_convert_fusion.3), channel_id=1, source_target_pairs={{0,8},{4,12},{8,0},{12,4},{16,24},{20,28},{24,16},{28,20},{1,9},{5... | collective-permute-start | bytes 786440 | tf_op jit(solution)/shard_map/ppermute | solution.py:243
  91.7 20.8 %collective-permute-start.30 = (bf16[1,16,4096]{2,1,0:T(8,128)(2,1)S(1)}, bf16[1,16,4096]{2,1,0:T(8,128)(2,1)S(1)}, u32[]{:S(2)}, u32[]{:S(2)}) collective-permute-start(bf16[1,16,4096]{2,1,0:T(8,128)(2,1)S(1)} %get-tuple-element.305), channel_id=1, source_target_pairs={{0,16},{4,20},{8,24},{12,28},{16,0},{20,4},{24,8},{28,12},{1,17},{... | collective-permute-start | bytes 393224 | tf_op jit(solution)/shard_map/ppermute | solution.py:243
  92.6 52.7 %collective-permute-start.37 = (bf16[4,16,4096]{2,1,0:T(8,128)(2,1)S(1)}, bf16[4,16,4096]{2,1,0:T(8,128)(2,1)S(1)}, u32[]{:S(2)}, u32[]{:S(2)}) collective-permute-start(bf16[4,16,4096]{2,1,0:T(8,128)(2,1)S(1)} %bitcast.112), channel_id=1, source_target_pairs={{0,4},{4,0},{8,12},{12,8},{16,20},{20,16},{24,28},{28,24},{1,5},{5... | collective-permute-start | bytes 1572872 | tf_op jit(solution)/shard_map/ppermute | solution.py:243
  98.1 12.0 %collective-permute-start.31 = (bf16[2,16,4096]{2,1,0:T(8,128)(2,1)S(1)}, bf16[2,16,4096]{2,1,0:T(8,128)(2,1)S(1)}, u32[]{:S(2)}, u32[]{:S(2)}) collective-permute-start(bf16[2,16,4096]{2,1,0:T(8,128)(2,1)S(1)} %add_convert_fusion.2), channel_id=1, source_target_pairs={{0,8},{4,12},{8,0},{12,4},{16,24},{20,28},{24,16},{28,20},{1,9},{5... | collective-permute-start | bytes 786440 | tf_op jit(solution)/shard_map/ppermute | solution.py:243
  107.4 17.1 %collective-permute-start.33 = (bf16[1,16,4096]{2,1,0:T(8,128)(2,1)S(1)}, bf16[1,16,4096]{2,1,0:T(8,128)(2,1)S(1)}, u32[]{:S(2)}, u32[]{:S(2)}) collective-permute-start(bf16[1,16,4096]{2,1,0:T(8,128)(2,1)S(1)} %get-tuple-element.310), channel_id=1, source_target_pairs={{0,16},{4,20},{8,24},{12,28},{16,0},{20,4},{24,8},{28,12},{1,17},{... | collective-permute-start | bytes 393224 | tf_op jit(solution)/shard_map/ppermute | solution.py:243
  110.2 14.2 %collective-permute-start.29 = (bf16[2,16,4096]{2,1,0:T(8,128)(2,1)S(1)}, bf16[2,16,4096]{2,1,0:T(8,128)(2,1)S(1)}, u32[]{:S(2)}, u32[]{:S(2)}) collective-permute-start(bf16[2,16,4096]{2,1,0:T(8,128)(2,1)S(1)} %add_convert_fusion.1), channel_id=1, source_target_pairs={{0,8},{4,12},{8,0},{12,4},{16,24},{20,28},{24,16},{28,20},{1,9},{5... | collective-permute-start | bytes 786440 | tf_op jit(solution)/shard_map/ppermute | solution.py:243
  110.3 21.0 %collective-permute-start.35 = (bf16[1,16,4096]{2,1,0:T(8,128)(2,1)S(1)}, bf16[1,16,4096]{2,1,0:T(8,128)(2,1)S(1)}, u32[]{:S(2)}, u32[]{:S(2)}) collective-permute-start(bf16[1,16,4096]{2,1,0:T(8,128)(2,1)S(1)} %add_convert_fusion.11), channel_id=1, source_target_pairs={{0,16},{4,20},{8,24},{12,28},{16,0},{20,4},{24,8},{28,12},{1,17},{... | collective-permute-start | bytes 393224 | tf_op jit(solution)/shard_map/ppermute | solution.py:243
  112.6 24.2 %collective-permute-start.38 = (bf16[2,16,4096]{2,1,0:T(8,128)(2,1)S(1)}, bf16[2,16,4096]{2,1,0:T(8,128)(2,1)S(1)}, u32[]{:S(2)}, u32[]{:S(2)}) collective-permute-start(bf16[2,16,4096]{2,1,0:T(8,128)(2,1)S(1)} %maximum_bitcast_fusion.5), channel_id=1, source_target_pairs={{0,8},{4,12},{8,0},{12,4},{16,24},{20,28},{24,16},{28,20},{1,9},{5... | collective-permute-start | bytes 786440 | tf_op jit(solution)/shard_map/ppermute | solution.py:243
  124.5 12.1 %collective-permute-start.39 = (bf16[2,16,4096]{2,1,0:T(8,128)(2,1)S(1)}, bf16[2,16,4096]{2,1,0:T(8,128)(2,1)S(1)}, u32[]{:S(2)}, u32[]{:S(2)}) collective-permute-start(bf16[2,16,4096]{2,1,0:T(8,128)(2,1)S(1)} %maximum_bitcast_fusion.6), channel_id=1, source_target_pairs={{0,8},{4,12},{8,0},{12,4},{16,24},{20,28},{24,16},{28,20},{1,9},{5... | collective-permute-start | bytes 786440 | tf_op jit(solution)/shard_map/ppermute | solution.py:243
  142.2 13.3 %collective-permute-start.45 = (bf16[1,16,4096]{2,1,0:T(8,128)(2,1)S(1)}, bf16[1,16,4096]{2,1,0:T(8,128)(2,1)S(1)}, u32[]{:S(2)}, u32[]{:S(2)}) collective-permute-start(bf16[1,16,4096]{2,1,0:T(8,128)(2,1)S(1)} %get-tuple-element.344), channel_id=1, source_target_pairs={{0,16},{4,20},{8,24},{12,28},{16,0},{20,4},{24,8},{28,12},{1,17},{... | collective-permute-start | bytes 393224 | tf_op jit(solution)/shard_map/ppermute | solution.py:243
  155.8 12.1 %collective-permute-start.46 = (bf16[2,384,512]{2,1,0:T(8,128)(2,1)S(1)}, bf16[2,384,512]{2,1,0:T(8,128)(2,1)S(1)}, u32[]{:S(2)}, u32[]{:S(2)}) collective-permute-start(bf16[2,384,512]{2,1,0:T(8,128)(2,1)S(1)} %get-tuple-element.352), channel_id=1, source_target_pairs={{0,1},{1,0},{2,3},{3,2},{4,6},{5,7},{6,4},{7,5},{8,9},{9,8},{10,11... | collective-permute-start | bytes 2359304 | tf_op jit(solution)/shard_map/ppermute | solution.py:240
  157.7 13.8 %collective-permute-start.50 = (bf16[4,16,4096]{2,1,0:T(8,128)(2,1)S(1)}, bf16[4,16,4096]{2,1,0:T(8,128)(2,1)S(1)}, u32[]{:S(2)}, u32[]{:S(2)}) collective-permute-start(bf16[4,16,4096]{2,1,0:T(8,128)(2,1)S(1)} %bitcast.106), channel_id=1, source_target_pairs={{0,4},{4,0},{8,12},{12,8},{16,20},{20,16},{24,28},{28,24},{1,5},{5... | collective-permute-start | bytes 1572872 | tf_op jit(solution)/shard_map/ppermute | solution.py:243
  168.0 22.3 %collective-permute-start.48 = (f32[1,384,512]{2,1,0:T(8,128)S(1)}, f32[1,384,512]{2,1,0:T(8,128)S(1)}, u32[]{:S(2)}, u32[]{:S(2)}) collective-permute-start(f32[1,384,512]{2,1,0:T(8,128)S(1)} %convert_add_fusion), channel_id=1, source_target_pairs={{0,2},{1,3},{2,0},{3,1},{4,5},{5,4},{6,7},{7,6},{8,10},{9,11},{10,... | collective-permute-start | bytes 2359304 | tf_op jit(solution)/shard_map/ppermute | solution.py:240
  189.7 12.0 %collective-permute-start.55 = (f32[1,256,512]{2,1,0:T(8,128)S(1)}, f32[1,256,512]{2,1,0:T(8,128)S(1)}, u32[]{:S(2)}, u32[]{:S(2)}) collective-permute-start(f32[1,256,512]{2,1,0:T(8,128)S(1)} %convert_add_fusion.1), channel_id=1, source_target_pairs={{0,2},{1,3},{2,0},{3,1},{4,5},{5,4},{6,7},{7,6},{8,10},{9,11},{10,... | collective-permute-start | bytes 1572872 | tf_op jit(solution)/shard_map/ppermute | solution.py:240
  (83 other events, 789.8 us)

commit v2 on v1

--- a/solution.py
+++ b/solution.py
@@ -15,7 +15,7 @@
     6: (
         ((1,), (1,), (1, 1), (1, 1)),
         ((0, 1, 2), (3, 4), (5,)),
-        (0, 3, 1, 0, 2, 0, 1, 0, 2, 1, 3, 4, 2, 4, 1, 3, 2, 4, 5, 3, 4, 5, 6, 4, 5, 6, 8, 5, 4, 6, 8, 7, 6, 7, 8, 5, 7, 6, 9, 8, 9, 7, 6, 5, 8, 10, 9, 7, 8, 9, 7, 10, 9, 11, 9, 12, 11, 10, 12, 11, 12),
+        (0, 1, 0, 0, 1, 0, 2, 1, 3, 4, 1, 2, 4, 5, 4, 2, 5, 2, 4, 5, 6, 4, 3, 6, 5, 7, 4, 3, 6, 7, 3, 6, 5, 8, 7, 8, 7, 6, 9, 8, 5, 9, 7, 6, 8, 9, 10, 7, 8, 9, 10, 9, 8, 9, 11, 10, 12, 11, 12, 11, 12),
     ),
 }
 
@@ -61,27 +61,30 @@
     tile = min(1024, D)
     first = off == 0
 
-    def body(info_ref, a_ref, res_ref, w_ref, keep, send, x, res, sems, *own):
-        copies = [
-            pltpu.make_async_copy(
-                a_ref.at[pl.ds(info_ref[3 + m] * span, span), off : off + r],
-                x.at[m * span : (m + 1) * span],
-                sems.at[m],
-            )
-            for m in range(F)
-        ]
-        copies.append(
-            pltpu.make_async_copy(
-                res_ref.at[pl.ds(info_ref[3] * span, span), off : off + r], res, sems.at[F]
-            )
+    def body(info_ref, res_ref, a_ref, w_ref, keep, send, x, res, sems, *own):
+        fetch = pltpu.make_async_copy(
+            res_ref.at[pl.ds(info_ref[3] * span, span), off : off + r], res, sems.at[F]
         )
+        fetch.start()
         if first:
+            copies = [
+                pltpu.make_async_copy(
+                    a_ref.at[pl.ds(info_ref[3 + m] * span, span), off : off + r],
+                    x.at[m * span : (m + 1) * span],
+                    sems.at[m],
+                )
+                for m in range(F)
+            ]
             copies.append(pltpu.make_async_copy(w_ref, own[0], sems.at[F + 1]))
             w_ref = own[0]
-        for copy in copies:
-            copy.start()
-        for copy in copies:
-            copy.wait()
+            for copy in copies:
+                copy.start()
+            for copy in copies:
+                copy.wait()
+        else:
+            for m in range(F):
+                x[m * span : (m + 1) * span] = a_ref[pl.ds(info_ref[3 + m] * span, span), off : off + r, :]
+        fetch.wait()
 
         @pl.loop(0, D // tile)
         def _(i):
@@ -101,10 +104,10 @@
         "project",
         body,
         [like(half, F32), like(half, BF16)],
+        residual,
         heads,
-        residual,
         weight,
-        far=3 if first else 2,
+        far=3 if first else 1,
         scratch=[
             pltpu.VMEM((F * span, r, K), BF16),
             pltpu.VMEM((span, r, D), BF16),

time: 206 us -> 198 us (0.961)
  waiting for transfers between devices: 83 us -> 75.2 us
    ppermute x22, waiting for transfers between devices: 39.5 us -> 34.4 us  [over_feat(): return lax.ppermute(a, ('layer', 'feat'), pairs)]
    ppermute x36, waiting for transfers between devices: 43.5 us -> 40.8 us  [over_layer(): return lax.ppermute(a, 'layer', [(l, l ^ 1 << s) for l in range(self.L)])]
  transfers between devices with their start and end apart: 58 -> 58, of which waited for: 26 -> 28; matrix products, arithmetic and copies ran while one was open for 2% -> 2% of each run, Pallas kernels for 24% -> 25%
where the time goes in v2:
time: 198 us
  waiting for transfers between devices  75.2 us (38%)
  starting transfers between devices  63 us (32%)
  Pallas kernels  52.1 us (26%)
  other arithmetic  2.7 us (1%)
  local copies, waits for them, and re-layouts  2.62 us (1%)
  between operations  2.06 us (1%)
    pallas_call x13, Pallas kernels, run(): pl.pallas_call(body, in_specs=[pl.BlockSpec(memory_space=pltpu.SMEM)] + [...  52.1 us
    ppermute x36, waiting for transfers between devices, over_layer(): return lax.ppermute(a, 'layer', [(l, l ^ 1 << s) for l in range(self.L)])  40.8 us
    ppermute x22, waiting for transfers between devices, over_feat(): return lax.ppermute(a, ('layer', 'feat'), pairs)  34.4 us
    ppermute x22, starting transfers between devices, over_feat(): return lax.ppermute(a, ('layer', 'feat'), pairs)  33 us
    ppermute x36, starting transfers between devices, over_layer(): return lax.ppermute(a, 'layer', [(l, l ^ 1 << s) for l in range(self.L)])  30 us
  transfers between devices with their start and end apart: 58, of which 28 were waited for; matrix products, arithmetic and copies ran while one was open for 2% of the time, Pallas kernels for 25%

profile of v2, /device:TPU:0, one launch (start us, length us, event | category | flops | bytes accessed | tf_op | source)
XLA Modules:
  0.0 197.7 jit_solution(18291609902928793823)
XLA Ops:
  0.7 3.2 %project.4 = (f32[2,32,2048]{2,1,0:T(8,128)S(1)}, bf16[2,32,2048]{2,1,0:T(8,128)(2,1)S(1)}) custom-call(s32[7]{0:T(128)S(1)} %stack.172.info_ref, bf16[8,96,2048]{2,1,0:T(8,128)(2,1)} %bitcast.120, bf16[8,96,512]{2,1,0:T(8,128)(2,1)} %bitcast.104, bf16[512,2048]{1,0:T(8,128)(2,1)} %bitcast.100), custom_call_target="tpu_custom_call" | custom-call | flops 268435456 | bytes 6815744 | tf_op jit(solution)/shard_map/project/pallas_call | solution.py:38
  4.0 3.0 %collective-permute-start = (bf16[2,32,2048]{2,1,0:T(8,128)(2,1)S(1)}, bf16[2,32,2048]{2,1,0:T(8,128)(2,1)S(1)}, u32[]{:S(2)}, u32[]{:S(2)}) collective-permute-start(bf16[2,32,2048]{2,1,0:T(8,128)(2,1)S(1)} %get-tuple-element.198), channel_id=1, source_target_pairs={{0,1},{1,0},{2,3},{3,2},{4,6},{5,7},{6,4},{7,5},{8,9},{9,8},{10,11... | collective-permute-start | bytes 786440 | tf_op jit(solution)/shard_map/ppermute | solution.py:243
  13.5 3.5 %collective-permute-done.3 = bf16[2,32,2048]{2,1,0:T(8,128)(2,1)S(1)} collective-permute-done((bf16[2,32,2048]{2,1,0:T(8,128)(2,1)S(1)}, bf16[2,32,2048]{2,1,0:T(8,128)(2,1)S(1)}, u32[]{:S(2)}, u32[]{:S(2)}) %collective-permute-start.3) | collective-permute-done | bytes 262176 | tf_op jit(solution)/shard_map/ppermute | solution.py:243
  19.2 2.8 %collective-permute-done.2 = bf16[1,32,2048]{2,1,0:T(8,128)(2,1)S(1)} collective-permute-done((bf16[1,32,2048]{2,1,0:T(8,128)(2,1)S(1)}, bf16[1,32,2048]{2,1,0:T(8,128)(2,1)S(1)}, u32[]{:S(2)}, u32[]{:S(2)}) %collective-permute-start.2) | collective-permute-done | bytes 131104 | tf_op jit(solution)/shard_map/ppermute | solution.py:243
  32.4 4.2 %encode.6 = (f32[4,16,4096]{2,1,0:T(8,128)S(1)}, bf16[4,16,4096]{2,1,0:T(8,128)(2,1)S(1)}) custom-call(s32[7]{0:T(128)S(1)} %stack.172.info_ref, bf16[2,32,2048]{2,1,0:T(8,128)(2,1)S(1)} %maximum_bitcast_fusion.2.near_ref, bf16[2,32,2048]{2,1,0:T(8,128)(2,1)S(1)} %collective-permute-done.4.far_ref, bf16[2048,4096]{1,0:T(8,128)(2,1)S(1)} %bitcast.89), custom_call_target="tpu_custom_call" | custom-call | flops 2147483648 | bytes 18874368 | tf_op jit(solution)/shard_map/encode/pallas_call | solution.py:38
  41.6 3.4 %collective-permute-done.10.far_ref = bf16[2,32,2048]{2,1,0:T(8,128)(2,1)S(1)} collective-permute-done((bf16[2,32,2048]{2,1,0:T(8,128)(2,1)S(1)}, bf16[2,32,2048]{2,1,0:T(8,128)(2,1)S(1)}, u32[]{:S(2)}, u32[]{:S(2)}) %collective-permute-start.10) | collective-permute-done | bytes 262176 | tf_op jit(solution)/shard_map/ppermute | solution.py:243
  45.0 4.2 %encode.7 = (f32[4,16,4096]{2,1,0:T(8,128)S(1)}, bf16[4,16,4096]{2,1,0:T(8,128)(2,1)S(1)}) custom-call(s32[7]{0:T(128)S(1)} %stack.172.info_ref, bf16[2,32,2048]{2,1,0:T(8,128)(2,1)S(1)} %maximum_bitcast_fusion.3.near_ref, bf16[2,32,2048]{2,1,0:T(8,128)(2,1)S(1)} %collective-permute-done.10.far_ref, bf16[2048,4096]{1,0:T(8,128)(2,1)S(1)} %bitcast.90), custom_call_target="tpu_custom_call" | custom-call | flops 2147483648 | bytes 18874368 | tf_op jit(solution)/shard_map/encode/pallas_call | solution.py:38
  62.0 4.0 %collective-permute-done.15 = bf16[2,16,4096]{2,1,0:T(8,128)(2,1)S(1)} collective-permute-done((bf16[2,16,4096]{2,1,0:T(8,128)(2,1)S(1)}, bf16[2,16,4096]{2,1,0:T(8,128)(2,1)S(1)}, u32[]{:S(2)}, u32[]{:S(2)}) %collective-permute-start.15) | collective-permute-done | bytes 262176 | tf_op jit(solution)/shard_map/ppermute | solution.py:246
  68.3 4.2 %encode.8 = (f32[4,16,4096]{2,1,0:T(8,128)S(1)}, bf16[4,16,4096]{2,1,0:T(8,128)(2,1)S(1)}) custom-call(s32[7]{0:T(128)S(1)} %stack.172.info_ref, bf16[2,64,2048]{2,1,0:T(8,128)(2,1)S(1)} %maximum_bitcast_fusion.near_ref, bf16[2,64,2048]{2,1,0:T(8,128)(2,1)S(1)} %collective-permute-done.17.far_ref, bf16[2048,4096]{1,0:T(8,128)(2,1)S(1)} %bitcast.91), custom_call_target="tpu_custom_call" | custom-call | flops 2147483648 | bytes 19398656 | tf_op jit(solution)/shard_map/encode/pallas_call | solution.py:38
  78.8 4.2 %encode.9 = (f32[4,16,4096]{2,1,0:T(8,128)S(1)}, bf16[4,16,4096]{2,1,0:T(8,128)(2,1)S(1)}) custom-call(s32[7]{0:T(128)S(1)} %stack.172.info_ref, bf16[2,64,2048]{2,1,0:T(8,128)(2,1)S(1)} %maximum_bitcast_fusion.near_ref, bf16[2,64,2048]{2,1,0:T(8,128)(2,1)S(1)} %collective-permute-done.17.far_ref, bf16[2048,4096]{1,0:T(8,128)(2,1)S(1)} %bitcast.92), custom_call_target="tpu_custom_call" | custom-call | flops 2147483648 | bytes 19398656 | tf_op jit(solution)/shard_map/encode/pallas_call | solution.py:38
  88.1 2.8 %collective-permute-done.21 = bf16[2,16,4096]{2,1,0:T(8,128)(2,1)S(1)} collective-permute-done((bf16[2,16,4096]{2,1,0:T(8,128)(2,1)S(1)}, bf16[2,16,4096]{2,1,0:T(8,128)(2,1)S(1)}, u32[]{:S(2)}, u32[]{:S(2)}) %collective-permute-start.21) | collective-permute-done | bytes 262176 | tf_op jit(solution)/shard_map/ppermute | solution.py:246
  95.8 4.0 %collective-permute-done.24 = bf16[1,16,4096]{2,1,0:T(8,128)(2,1)S(1)} collective-permute-done((bf16[1,16,4096]{2,1,0:T(8,128)(2,1)S(1)}, bf16[1,16,4096]{2,1,0:T(8,128)(2,1)S(1)}, u32[]{:S(2)}, u32[]{:S(2)}) %collective-permute-start.24) | collective-permute-done | bytes 131104 | tf_op jit(solution)/shard_map/ppermute | solution.py:246
  103.4 4.2 %encode.10 = (f32[4,16,4096]{2,1,0:T(8,128)S(1)}, bf16[4,16,4096]{2,1,0:T(8,128)(2,1)S(1)}) custom-call(s32[7]{0:T(128)S(1)} %stack.172.info_ref, bf16[2,64,2048]{2,1,0:T(8,128)(2,1)S(1)} %maximum_bitcast_fusion.1.near_ref, bf16[2,64,2048]{2,1,0:T(8,128)(2,1)S(1)} %collective-permute-done.28.far_ref, bf16[2048,4096]{1,0:T(8,128)(2,1)S(1)} %bitcast.93), custom_call_target="tpu_custom_call" | custom-call | flops 2147483648 | bytes 19398656 | tf_op jit(solution)/shard_map/encode/pallas_call | solution.py:38
  110.1 7.0 %collective-permute-done.30 = bf16[1,16,4096]{2,1,0:T(8,128)(2,1)S(1)} collective-permute-done((bf16[1,16,4096]{2,1,0:T(8,128)(2,1)S(1)}, bf16[1,16,4096]{2,1,0:T(8,128)(2,1)S(1)}, u32[]{:S(2)}, u32[]{:S(2)}) %collective-permute-start.30) | collective-permute-done | bytes 131104 | tf_op jit(solution)/shard_map/ppermute | solution.py:246
  119.7 4.4 %encode.11 = (f32[4,16,4096]{2,1,0:T(8,128)S(1)}, bf16[4,16,4096]{2,1,0:T(8,128)(2,1)S(1)}) custom-call(s32[7]{0:T(128)S(1)} %stack.172.info_ref, bf16[2,64,2048]{2,1,0:T(8,128)(2,1)S(1)} %maximum_bitcast_fusion.1.near_ref, bf16[2,64,2048]{2,1,0:T(8,128)(2,1)S(1)} %collective-permute-done.28.far_ref, bf16[2048,4096]{1,0:T(8,128)(2,1)S(1)} %bitcast.94), custom_call_target="tpu_custom_call" | custom-call | flops 2147483648 | bytes 19398656 | tf_op jit(solution)/shard_map/encode/pallas_call | solution.py:38
  129.6 4.5 %collective-permute-done.34 = bf16[1,16,4096]{2,1,0:T(8,128)(2,1)S(1)} collective-permute-done((bf16[1,16,4096]{2,1,0:T(8,128)(2,1)S(1)}, bf16[1,16,4096]{2,1,0:T(8,128)(2,1)S(1)}, u32[]{:S(2)}, u32[]{:S(2)}) %collective-permute-start.34) | collective-permute-done | bytes 131104 | tf_op jit(solution)/shard_map/ppermute | solution.py:246
  134.3 5.0 %collective-permute-done.39 = bf16[2,16,4096]{2,1,0:T(8,128)(2,1)S(1)} collective-permute-done((bf16[2,16,4096]{2,1,0:T(8,128)(2,1)S(1)}, bf16[2,16,4096]{2,1,0:T(8,128)(2,1)S(1)}, u32[]{:S(2)}, u32[]{:S(2)}) %collective-permute-start.39) | collective-permute-done | bytes 262176 | tf_op jit(solution)/shard_map/ppermute | solution.py:246
  142.3 7.7 %decode.3 = (f32[2,384,512]{2,1,0:T(8,128)S(1)}, bf16[2,384,512]{2,1,0:T(8,128)(2,1)S(1)}) custom-call(s32[7]{0:T(128)S(1)} %stack.172.info_ref, bf16[4,16,4096]{2,1,0:T(8,128)(2,1)S(1)} %bitcast.115, bf16[4,16,4096]{2,1,0:T(8,128)(2,1)S(1)} %collective-permute-done.43.refs_1_, bf16[4,16,4096]{2,1,0:T(8,128)(2,1)S(1)} %bitcast.117, ...), custom_call_target="tpu_custom_call" | custom-call | flops 6442450944 | bytes 22282240 | tf_op jit(solution)/shard_map/decode/pallas_call | solution.py:38
  154.8 8.8 %collective-permute-done.46 = bf16[2,384,512]{2,1,0:T(8,128)(2,1)S(1)} collective-permute-done((bf16[2,384,512]{2,1,0:T(8,128)(2,1)S(1)}, bf16[2,384,512]{2,1,0:T(8,128)(2,1)S(1)}, u32[]{:S(2)}, u32[]{:S(2)}) %collective-permute-start.46) | collective-permute-done | bytes 786464 | tf_op jit(solution)/shard_map/ppermute | solution.py:243
  166.9 3.8 %collective-permute-done.52 = bf16[2,16,4096]{2,1,0:T(8,128)(2,1)S(1)} collective-permute-done((bf16[2,16,4096]{2,1,0:T(8,128)(2,1)S(1)}, bf16[2,16,4096]{2,1,0:T(8,128)(2,1)S(1)}, u32[]{:S(2)}, u32[]{:S(2)}) %collective-permute-start.52) | collective-permute-done | bytes 262176 | tf_op jit(solution)/shard_map/ppermute | solution.py:246
  170.9 5.4 %decode.4 = (f32[2,256,512]{2,1,0:T(8,128)S(1)}, bf16[2,256,512]{2,1,0:T(8,128)(2,1)S(1)}) custom-call(s32[7]{0:T(128)S(1)} %stack.172.info_ref, bf16[4,16,4096]{2,1,0:T(8,128)(2,1)S(1)} %bitcast.109, bf16[4,16,4096]{2,1,0:T(8,128)(2,1)S(1)} %collective-permute-done.48.refs_1_, bf16[4,16,4096]{2,1,0:T(8,128)(2,1)S(1)} %bitcast.111, ...), custom_call_target="tpu_custom_call" | custom-call | flops 4294967296 | bytes 20447232 | tf_op jit(solution)/shard_map/decode/pallas_call | solution.py:38
  178.7 3.2 %decode.5 = (f32[2,128,512]{2,1,0:T(8,128)S(1)}, bf16[2,128,512]{2,1,0:T(8,128)(2,1)S(1)}) custom-call(s32[7]{0:T(128)S(1)} %stack.172.info_ref, bf16[4,16,4096]{2,1,0:T(8,128)(2,1)S(1)} %bitcast.113, bf16[4,16,4096]{2,1,0:T(8,128)(2,1)S(1)} %collective-permute-done.54.refs_1_, bf16[4096,2048]{1,0:T(8,128)(2,1)S(1)} %bitcast.99), custom_call_target="tpu_custom_call" | custom-call | flops 2147483648 | bytes 18612224 | tf_op jit(solution)/shard_map/decode/pallas_call | solution.py:38
  182.5 3.2 %collective-permute-done.53 = bf16[2,256,512]{2,1,0:T(8,128)(2,1)S(1)} collective-permute-done((bf16[2,256,512]{2,1,0:T(8,128)(2,1)S(1)}, bf16[2,256,512]{2,1,0:T(8,128)(2,1)S(1)}, u32[]{:S(2)}, u32[]{:S(2)}) %collective-permute-start.53) | collective-permute-done | bytes 524320 | tf_op jit(solution)/shard_map/ppermute | solution.py:243
  190.5 4.5 %collective-permute-done.55 = f32[1,256,512]{2,1,0:T(8,128)S(1)} collective-permute-done((f32[1,256,512]{2,1,0:T(8,128)S(1)}, f32[1,256,512]{2,1,0:T(8,128)S(1)}, u32[]{:S(2)}, u32[]{:S(2)}) %collective-permute-start.55) | collective-permute-done | bytes 524320 | tf_op jit(solution)/shard_map/ppermute | solution.py:243
  (298 shorter events, 90.3 us)
Async XLA Ops:
  26.1 11.3 %collective-permute-start.7 = (bf16[2,64,2048]{2,1,0:T(8,128)(2,1)S(1)}, bf16[2,64,2048]{2,1,0:T(8,128)(2,1)S(1)}, u32[]{:S(2)}, u32[]{:S(2)}) collective-permute-start(bf16[2,64,2048]{2,1,0:T(8,128)(2,1)S(1)} %get-tuple-element.229), channel_id=1, source_target_pairs={{0,1},{1,0},{2,3},{3,2},{4,6},{5,7},{6,4},{7,5},{8,9},{9,8},{10,11... | collective-permute-start | bytes 1572872 | tf_op jit(solution)/shard_map/ppermute | solution.py:243
  40.4 11.7 %collective-permute-start.12 = (f32[1,64,2048]{2,1,0:T(8,128)S(1)}, f32[1,64,2048]{2,1,0:T(8,128)S(1)}, u32[]{:S(2)}, u32[]{:S(2)}) collective-permute-start(f32[1,64,2048]{2,1,0:T(8,128)S(1)} %convert_add_fusion.3), channel_id=1, source_target_pairs={{0,2},{1,3},{2,0},{3,1},{4,5},{5,4},{6,7},{7,6},{8,10},{9,11},{10,... | collective-permute-start | bytes 1572872 | tf_op jit(solution)/shard_map/ppermute | solution.py:243
  49.5 11.7 %collective-permute-start.11 = (bf16[1,16,4096]{2,1,0:T(8,128)(2,1)S(1)}, bf16[1,16,4096]{2,1,0:T(8,128)(2,1)S(1)}, u32[]{:S(2)}, u32[]{:S(2)}) collective-permute-start(bf16[1,16,4096]{2,1,0:T(8,128)(2,1)S(1)} %add_convert_fusion.14), channel_id=1, source_target_pairs={{0,16},{4,20},{8,24},{12,28},{16,0},{20,4},{24,8},{28,12},{1,17},{... | collective-permute-start | bytes 393224 | tf_op jit(solution)/shard_map/ppermute | solution.py:246
  54.4 11.6 %collective-permute-start.15 = (bf16[2,16,4096]{2,1,0:T(8,128)(2,1)S(1)}, bf16[2,16,4096]{2,1,0:T(8,128)(2,1)S(1)}, u32[]{:S(2)}, u32[]{:S(2)}) collective-permute-start(bf16[2,16,4096]{2,1,0:T(8,128)(2,1)S(1)} %add_convert_fusion.5), channel_id=1, source_target_pairs={{0,8},{4,12},{8,0},{12,4},{16,24},{20,28},{24,16},{28,20},{1,9},{5... | collective-permute-start | bytes 786440 | tf_op jit(solution)/shard_map/ppermute | solution.py:246
  61.2 12.2 %collective-permute-start.20 = (bf16[1,16,4096]{2,1,0:T(8,128)(2,1)S(1)}, bf16[1,16,4096]{2,1,0:T(8,128)(2,1)S(1)}, u32[]{:S(2)}, u32[]{:S(2)}) collective-permute-start(bf16[1,16,4096]{2,1,0:T(8,128)(2,1)S(1)} %get-tuple-element.264), channel_id=1, source_target_pairs={{0,16},{4,20},{8,24},{12,28},{16,0},{20,4},{24,8},{28,12},{1,17},{... | collective-permute-start | bytes 393224 | tf_op jit(solution)/shard_map/ppermute | solution.py:246
  66.0 11.8 %collective-permute-start.16 = (bf16[1,16,4096]{2,1,0:T(8,128)(2,1)S(1)}, bf16[1,16,4096]{2,1,0:T(8,128)(2,1)S(1)}, u32[]{:S(2)}, u32[]{:S(2)}) collective-permute-start(bf16[1,16,4096]{2,1,0:T(8,128)(2,1)S(1)} %add_convert_fusion.13), channel_id=1, source_target_pairs={{0,16},{4,20},{8,24},{12,28},{16,0},{20,4},{24,8},{28,12},{1,17},{... | collective-permute-start | bytes 393224 | tf_op jit(solution)/shard_map/ppermute | solution.py:246
  73.6 12.1 %collective-permute-start.23 = (bf16[2,16,4096]{2,1,0:T(8,128)(2,1)S(1)}, bf16[2,16,4096]{2,1,0:T(8,128)(2,1)S(1)}, u32[]{:S(2)}, u32[]{:S(2)}) collective-permute-start(bf16[2,16,4096]{2,1,0:T(8,128)(2,1)S(1)} %maximum_bitcast_fusion.4), channel_id=1, source_target_pairs={{0,8},{4,12},{8,0},{12,4},{16,24},{20,28},{24,16},{28,20},{1,9},{5... | collective-permute-start | bytes 786440 | tf_op jit(solution)/shard_map/ppermute | solution.py:246
  77.7 13.2 %collective-permute-start.21 = (bf16[2,16,4096]{2,1,0:T(8,128)(2,1)S(1)}, bf16[2,16,4096]{2,1,0:T(8,128)(2,1)S(1)}, u32[]{:S(2)}, u32[]{:S(2)}) collective-permute-start(bf16[2,16,4096]{2,1,0:T(8,128)(2,1)S(1)} %add_convert_fusion.4), channel_id=1, source_target_pairs={{0,8},{4,12},{8,0},{12,4},{16,24},{20,28},{24,16},{28,20},{1,9},{5... | collective-permute-start | bytes 786440 | tf_op jit(solution)/shard_map/ppermute | solution.py:246
  77.9 21.9 %collective-permute-start.29 = (bf16[1,16,4096]{2,1,0:T(8,128)(2,1)S(1)}, bf16[1,16,4096]{2,1,0:T(8,128)(2,1)S(1)}, u32[]{:S(2)}, u32[]{:S(2)}) collective-permute-start(bf16[1,16,4096]{2,1,0:T(8,128)(2,1)S(1)} %get-tuple-element.295), channel_id=1, source_target_pairs={{0,16},{4,20},{8,24},{12,28},{16,0},{20,4},{24,8},{28,12},{1,17},{... | collective-permute-start | bytes 393224 | tf_op jit(solution)/shard_map/ppermute | solution.py:246
  85.7 53.8 %collective-permute-start.43 = (bf16[4,16,4096]{2,1,0:T(8,128)(2,1)S(1)}, bf16[4,16,4096]{2,1,0:T(8,128)(2,1)S(1)}, u32[]{:S(2)}, u32[]{:S(2)}) collective-permute-start(bf16[4,16,4096]{2,1,0:T(8,128)(2,1)S(1)} %bitcast.114), channel_id=1, source_target_pairs={{0,4},{4,0},{8,12},{12,8},{16,20},{20,16},{24,28},{28,24},{1,5},{5... | collective-permute-start | bytes 1572872 | tf_op jit(solution)/shard_map/ppermute | solution.py:246
  91.6 11.3 %collective-permute-start.27 = (bf16[2,16,4096]{2,1,0:T(8,128)(2,1)S(1)}, bf16[2,16,4096]{2,1,0:T(8,128)(2,1)S(1)}, u32[]{:S(2)}, u32[]{:S(2)}) collective-permute-start(bf16[2,16,4096]{2,1,0:T(8,128)(2,1)S(1)} %add_convert_fusion.2), channel_id=1, source_target_pairs={{0,8},{4,12},{8,0},{12,4},{16,24},{20,28},{24,16},{28,20},{1,9},{5... | collective-permute-start | bytes 786440 | tf_op jit(solution)/shard_map/ppermute | solution.py:246
  99.9 17.4 %collective-permute-start.33 = (bf16[1,16,4096]{2,1,0:T(8,128)(2,1)S(1)}, bf16[1,16,4096]{2,1,0:T(8,128)(2,1)S(1)}, u32[]{:S(2)}, u32[]{:S(2)}) collective-permute-start(bf16[1,16,4096]{2,1,0:T(8,128)(2,1)S(1)} %get-tuple-element.311), channel_id=1, source_target_pairs={{0,16},{4,20},{8,24},{12,28},{16,0},{20,4},{24,8},{28,12},{1,17},{... | collective-permute-start | bytes 393224 | tf_op jit(solution)/shard_map/ppermute | solution.py:246
  100.0 24.5 %collective-permute-start.38 = (bf16[2,16,4096]{2,1,0:T(8,128)(2,1)S(1)}, bf16[2,16,4096]{2,1,0:T(8,128)(2,1)S(1)}, u32[]{:S(2)}, u32[]{:S(2)}) collective-permute-start(bf16[2,16,4096]{2,1,0:T(8,128)(2,1)S(1)} %maximum_bitcast_fusion.5), channel_id=1, source_target_pairs={{0,8},{4,12},{8,0},{12,4},{16,24},{20,28},{24,16},{28,20},{1,9},{5... | collective-permute-start | bytes 786440 | tf_op jit(solution)/shard_map/ppermute | solution.py:246
  109.7 14.7 %collective-permute-start.32 = (bf16[2,16,4096]{2,1,0:T(8,128)(2,1)S(1)}, bf16[2,16,4096]{2,1,0:T(8,128)(2,1)S(1)}, u32[]{:S(2)}, u32[]{:S(2)}) collective-permute-start(bf16[2,16,4096]{2,1,0:T(8,128)(2,1)S(1)} %add_convert_fusion.1), channel_id=1, source_target_pairs={{0,8},{4,12},{8,0},{12,4},{16,24},{20,28},{24,16},{28,20},{1,9},{5... | collective-permute-start | bytes 786440 | tf_op jit(solution)/shard_map/ppermute | solution.py:246
  117.3 12.1 %collective-permute-start.35 = (bf16[2,16,4096]{2,1,0:T(8,128)(2,1)S(1)}, bf16[2,16,4096]{2,1,0:T(8,128)(2,1)S(1)}, u32[]{:S(2)}, u32[]{:S(2)}) collective-permute-start(bf16[2,16,4096]{2,1,0:T(8,128)(2,1)S(1)} %maximum_bitcast_fusion.6), channel_id=1, source_target_pairs={{0,8},{4,12},{8,0},{12,4},{16,24},{20,28},{24,16},{28,20},{1,9},{5... | collective-permute-start | bytes 786440 | tf_op jit(solution)/shard_map/ppermute | solution.py:246
  126.4 15.9 %collective-permute-start.44 = (bf16[4,16,4096]{2,1,0:T(8,128)(2,1)S(1)}, bf16[4,16,4096]{2,1,0:T(8,128)(2,1)S(1)}, u32[]{:S(2)}, u32[]{:S(2)}) collective-permute-start(bf16[4,16,4096]{2,1,0:T(8,128)(2,1)S(1)} %bitcast.116), channel_id=1, source_target_pairs={{0,4},{4,0},{8,12},{12,8},{16,20},{20,16},{24,28},{28,24},{1,5},{5... | collective-permute-start | bytes 1572872 | tf_op jit(solution)/shard_map/ppermute | solution.py:246
  126.7 12.6 %collective-permute-start.39 = (bf16[2,16,4096]{2,1,0:T(8,128)(2,1)S(1)}, bf16[2,16,4096]{2,1,0:T(8,128)(2,1)S(1)}, u32[]{:S(2)}, u32[]{:S(2)}) collective-permute-start(bf16[2,16,4096]{2,1,0:T(8,128)(2,1)S(1)} %add_convert_fusion), channel_id=1, source_target_pairs={{0,8},{4,12},{8,0},{12,4},{16,24},{20,28},{24,16},{28,20},{1,9},{5... | collective-permute-start | bytes 786440 | tf_op jit(solution)/shard_map/ppermute | solution.py:246
  129.4 20.7 %collective-permute-start.42 = (bf16[2,16,4096]{2,1,0:T(8,128)(2,1)S(1)}, bf16[2,16,4096]{2,1,0:T(8,128)(2,1)S(1)}, u32[]{:S(2)}, u32[]{:S(2)}) collective-permute-start(bf16[2,16,4096]{2,1,0:T(8,128)(2,1)S(1)} %maximum_bitcast_fusion.7), channel_id=1, source_target_pairs={{0,8},{4,12},{8,0},{12,4},{16,24},{20,28},{24,16},{28,20},{1,9},{5... | collective-permute-start | bytes 786440 | tf_op jit(solution)/shard_map/ppermute | solution.py:246
  139.2 11.1 %collective-permute-start.41 = (bf16[1,16,4096]{2,1,0:T(8,128)(2,1)S(1)}, bf16[1,16,4096]{2,1,0:T(8,128)(2,1)S(1)}, u32[]{:S(2)}, u32[]{:S(2)}) collective-permute-start(bf16[1,16,4096]{2,1,0:T(8,128)(2,1)S(1)} %get-tuple-element.346), channel_id=1, source_target_pairs={{0,16},{4,20},{8,24},{12,28},{16,0},{20,4},{24,8},{28,12},{1,17},{... | collective-permute-start | bytes 393224 | tf_op jit(solution)/shard_map/ppermute | solution.py:246
  139.6 12.0 %collective-permute-start.40 = (bf16[1,16,4096]{2,1,0:T(8,128)(2,1)S(1)}, bf16[1,16,4096]{2,1,0:T(8,128)(2,1)S(1)}, u32[]{:S(2)}, u32[]{:S(2)}) collective-permute-start(bf16[1,16,4096]{2,1,0:T(8,128)(2,1)S(1)} %add_convert_fusion.9), channel_id=1, source_target_pairs={{0,16},{4,20},{8,24},{12,28},{16,0},{20,4},{24,8},{28,12},{1,17},{... | collective-permute-start | bytes 393224 | tf_op jit(solution)/shard_map/ppermute | solution.py:246
  150.2 20.7 %collective-permute-start.48 = (bf16[4,16,4096]{2,1,0:T(8,128)(2,1)S(1)}, bf16[4,16,4096]{2,1,0:T(8,128)(2,1)S(1)}, u32[]{:S(2)}, u32[]{:S(2)}) collective-permute-start(bf16[4,16,4096]{2,1,0:T(8,128)(2,1)S(1)} %bitcast.108), channel_id=1, source_target_pairs={{0,4},{4,0},{8,12},{12,8},{16,20},{20,16},{24,28},{28,24},{1,5},{5... | collective-permute-start | bytes 1572872 | tf_op jit(solution)/shard_map/ppermute | solution.py:246
  150.4 14.3 %collective-permute-start.49 = (bf16[2,16,4096]{2,1,0:T(8,128)(2,1)S(1)}, bf16[2,16,4096]{2,1,0:T(8,128)(2,1)S(1)}, u32[]{:S(2)}, u32[]{:S(2)}) collective-permute-start(bf16[2,16,4096]{2,1,0:T(8,128)(2,1)S(1)} %maximum_bitcast_fusion.8), channel_id=1, source_target_pairs={{0,8},{4,12},{8,0},{12,4},{16,24},{20,28},{24,16},{28,20},{1,9},{5... | collective-permute-start | bytes 786440 | tf_op jit(solution)/shard_map/ppermute | solution.py:246
  151.6 12.0 %collective-permute-start.46 = (bf16[2,384,512]{2,1,0:T(8,128)(2,1)S(1)}, bf16[2,384,512]{2,1,0:T(8,128)(2,1)S(1)}, u32[]{:S(2)}, u32[]{:S(2)}) collective-permute-start(bf16[2,384,512]{2,1,0:T(8,128)(2,1)S(1)} %get-tuple-element.352), channel_id=1, source_target_pairs={{0,1},{1,0},{2,3},{3,2},{4,6},{5,7},{6,4},{7,5},{8,9},{9,8},{10,11... | collective-permute-start | bytes 2359304 | tf_op jit(solution)/shard_map/ppermute | solution.py:243
  165.0 13.5 %collective-permute-start.47 = (f32[1,384,512]{2,1,0:T(8,128)S(1)}, f32[1,384,512]{2,1,0:T(8,128)S(1)}, u32[]{:S(2)}, u32[]{:S(2)}) collective-permute-start(f32[1,384,512]{2,1,0:T(8,128)S(1)} %convert_add_fusion), channel_id=1, source_target_pairs={{0,2},{1,3},{2,0},{3,1},{4,5},{5,4},{6,7},{7,6},{8,10},{9,11},{10,... | collective-permute-start | bytes 2359304 | tf_op jit(solution)/shard_map/ppermute | solution.py:243
  (83 other events, 741.9 us)
